TPU v7x, 128 devices: a whole 4x4x4 slice. The times are simulated.
128 devices in a mesh: grp: 16 (over y, x), loc: 8 (over z, core).
Axes of the slice: x: 4, y: 4, z: 4, core: 2. Of those that a mesh axis runs over, the one named last changes fastest.
Arguments:
- stream_in: bfloat16 [16384, 3584], P(('grp', 'loc')), may hold values from -6 to 6
- norm_gain: float32 [3584], replicated, may hold values from 0.1 to 1.9
- shared_gate: bfloat16 [3584, 1024], P('grp', 'loc'), may hold values from -0.09375 to 0.09375
- shared_up: bfloat16 [3584, 1024], P('grp', 'loc'), may hold values from -0.09375 to 0.09375
- shared_down: bfloat16 [1024, 3584], P('loc', 'grp'), may hold values from -0.1875 to 0.1875
- expert_gate: bfloat16 [128, 3584, 1024], P(('grp', 'loc')), may hold values from -0.09375 to 0.09375
- expert_up: bfloat16 [128, 3584, 1024], P(('grp', 'loc')), may hold values from -0.09375 to 0.09375
- expert_down: bfloat16 [128, 1024, 3584], P(('grp', 'loc')), may hold values from -0.1875 to 0.1875
- expert_ids: int32 [16384, 8], P(('grp', 'loc')), may hold values from 0 to 127, as said below
- gate_weights: bfloat16 [16384, 8], P(('grp', 'loc')), may hold values from 0.049804688 to 0.5
- cotangent: bfloat16 [16384, 3584], P(('grp', 'loc')), may hold values from -0.100097656 to 0.100097656
Outputs:
- layer_out: bfloat16 [16384, 3584], P(('grp', 'loc'))
- gate_grads: float32 [16384, 8], P(('grp', 'loc'))
Inputs may be any that keep to these rules, and one draw needn't show every extreme that they name: `expert_ids`: each token names 8 different experts, two from each of exactly 4 groups, a group being 8 consecutive experts. Among the 128 tokens of one device (aligned blocks of rows), every group is named by exactly 32 tokens and no expert by more than 9; in every group one expert is named by exactly 9 tokens of every device.
All inputs are finite; a program needn't handle non-finite values.
Results may differ from a plain program's by a relative error of at most 0.015.
Values may be sent and summed in bfloat16 or wider, within the bound.
A program may use at most 192 MiB of HBM per device.

v0:
```python
import jax
import jax.numpy as jnp
from jax import lax
from jax.sharding import PartitionSpec as P

epsilon = 1e-06


def swiglu_rows(inputs, w_gate, w_up, w_down):
    gate_act = jnp.dot(inputs, w_gate, preferred_element_type=jnp.float32)
    up_act = jnp.dot(inputs, w_up, preferred_element_type=jnp.float32)
    hidden = (jax.nn.silu(gate_act) * up_act).astype(jnp.bfloat16)
    return jnp.dot(hidden, w_down, preferred_element_type=jnp.float32)


def body(
    stream_in,
    norm_gain,
    shared_gate,
    shared_up,
    shared_down,
    expert_gate,
    expert_up,
    expert_down,
    expert_ids,
    gate_weights,
    cotangent,
):
    groups = lax.axis_size("grp")
    members = lax.axis_size("loc")
    experts = groups * members
    tok_dev, model_width = cotangent.shape
    top_count = expert_ids.shape[1]
    bf_zero = jnp.zeros((), jnp.bfloat16)
    values = stream_in.astype(jnp.float32)
    inverse_rms = lax.rsqrt(jnp.mean(values * values, axis=1, keepdims=True) + epsilon)
    normed = (values * inverse_rms * norm_gain).astype(jnp.bfloat16)
    gate_full, up_full, down_full = (
        lax.all_gather(shared_gate, "grp", axis=0, tiled=True),
        lax.all_gather(shared_up, "grp", axis=0, tiled=True),
        lax.all_gather(shared_down, "grp", axis=1, tiled=True),
    )
    piece = lax.all_gather(normed, "loc", axis=0, tiled=True)
    shared_act = jnp.dot(piece, gate_full, preferred_element_type=jnp.float32)
    shared_lift = jnp.dot(piece, up_full, preferred_element_type=jnp.float32)
    shared_hidden = (jax.nn.silu(shared_act) * shared_lift).astype(jnp.bfloat16)
    shared_out = lax.psum_scatter(
        jnp.dot(shared_hidden, down_full, preferred_element_type=jnp.float32).astype(jnp.bfloat16),
        "loc",
        scatter_dimension=0,
        tiled=True,
    ).astype(jnp.float32)
    pair_count = tok_dev * top_count
    flat_ids = expert_ids.reshape(pair_count)
    pair_token = jnp.arange(pair_count, dtype=jnp.int32) // top_count
    slot_count = 9 * tok_dev // experts
    expert_hits = (flat_ids[:, None] == jnp.arange(experts, dtype=jnp.int32)[None, :]).astype(
        jnp.int32
    )
    rank_flat = jnp.sum((jnp.cumsum(expert_hits, axis=0) - 1) * expert_hits, axis=1)
    slot_of_pair = flat_ids * slot_count + rank_flat
    slot_token = (
        jnp.full((experts * slot_count,), -1, jnp.int32)
        .at[slot_of_pair]
        .set(pair_token, mode="drop")
    )
    slot_filled = slot_token >= 0
    outgoing = jnp.where(slot_filled[:, None], normed[jnp.maximum(slot_token, 0)], bf_zero)
    outgoing = outgoing.reshape(experts, slot_count, model_width)
    parcel = lax.all_to_all(outgoing, ("grp", "loc"), split_axis=0, concat_axis=0, tiled=True)
    outcome = (
        swiglu_rows(parcel.reshape(-1, model_width), expert_gate[0], expert_up[0], expert_down[0])
        .astype(jnp.bfloat16)
        .reshape(parcel.shape)
    )
    returned = lax.all_to_all(outcome, ("grp", "loc"), split_axis=0, concat_axis=0, tiled=True)
    picked = returned.reshape(experts * slot_count, model_width)[slot_of_pair].reshape(
        tok_dev, top_count, model_width
    )
    routed = jnp.einsum("tk,tkd->td", gate_weights, picked, preferred_element_type=jnp.float32)
    gate_grads = jnp.einsum("tkd,td->tk", picked, cotangent, preferred_element_type=jnp.float32)
    layer_out = (shared_out + routed).astype(jnp.bfloat16)
    return (layer_out, gate_grads)


def solution(mesh):
    placed = (
        P(("grp", "loc"), None),
        P(),
        P("grp", "loc"),
        P("grp", "loc"),
        P("loc", "grp"),
        P(("grp", "loc"), None, None),
        P(("grp", "loc"), None, None),
        P(("grp", "loc"), None, None),
        P(("grp", "loc"), None),
        P(("grp", "loc"), None),
        P(("grp", "loc"), None),
    )
    return jax.shard_map(
        body,
        mesh=mesh,
        in_specs=placed,
        out_specs=(P(("grp", "loc"), None), P(("grp", "loc"), None)),
        check_vma=False,
    )
```

profile of v0, /device:TPU:1, one launch (start us, length us, event | category | flops | bytes accessed | tf_op | source)
XLA Modules:
  0.0 673.3 jit_solution(5604729186328362951)
XLA Ops:
  7.2 1.5 fusion.15
  8.8 2.4 fusion.17
  11.2 0.9 copy.14
  12.3 0.2 fusion.22
  12.7 0.7 broadcast_multiply_fusion
  13.4 0.1 copy.13
  13.6 0.4 fusion.21
  14.0 4.3 scatter_custom_fusion
  18.4 7.5 %gather_fusion = bf16[1152,3584]{1,0:T(8,128)(2,1)} fusion(bf16[128,3584]{1,0:T(8,128)(2,1)S(1)} %copy-done.1, s32[2048]{0:T(1024)S(1)} %pad_clamp_fusion), kind=kCustom, calls=%fused_computation | custom fusion | bytes 16519680 | tf_op jit(solution)/shard_map/gather | solution.py:68
  25.9 14.3 %gather.9 = bf16[128,9,3584]{2,1,0:T(8,128)(2,1)} reshape(bf16[1152,3584]{1,0:T(8,128)(2,1)} %gather_fusion) | data formatting | bytes 16515072 | tf_op jit(solution)/shard_map/gather | solution.py:68
  40.2 0.2 broadcast_in_dim.27
  40.4 11.1 %broadcast_select_fusion = bf16[128,9,3584]{2,1,0:T(8,128)(2,1)} fusion(bf16[128,9,3584]{2,1,0:T(8,128)(2,1)} %gather.9, pred[128,9]{1,0:T(8,128)(4,1)S(1)} %broadcast_in_dim.27), kind=kLoop, calls=%fused_computation.4 | loop fusion | flops 4128768 | bytes 16516224 | tf_op jit(solution)/shard_map/jit(_where)/select_n | solution.py:68
  51.6 11.8 %all-to-all-start = ((bf16[128,9,3584]{2,1,0:T(8,128)(2,1)}), bf16[128,9,3584]{2,1,0:T(8,128)(2,1)}, u32[]{:S(2)}, u32[]{:S(2)}) async-start(bf16[128,9,3584]{2,1,0:T(8,128)(2,1)} %broadcast_select_fusion), calls=%async_computation.1 | async-start | bytes 29360128 | tf_op jit(solution)/shard_map/all_to_all | solution.py:70
  63.4 206.3 %all_gather.13 = bf16[3584,128]{1,0:T(8,128)(2,1)} all-gather(bf16[224,128]{1,0:T(8,128)(2,1)S(1)} %copy-done.2), channel_id=1, replica_groups=mesh['grp'=16,'loc'=8] {'grp'}, dimensions={0}, use_global_device_ids=true | all-gather | bytes 974848 | tf_op jit(solution)/shard_map/all_gather | solution.py:39
  269.7 17.0 %all_gather.14 = bf16[3584,128]{1,0:T(8,128)(2,1)S(1)} all-gather(bf16[224,128]{1,0:T(8,128)(2,1)S(1)} %copy-done.3), channel_id=1, replica_groups=mesh['grp'=16,'loc'=8] {'grp'}, dimensions={0}, use_global_device_ids=true | all-gather | bytes 974848 | tf_op jit(solution)/shard_map/all_gather | solution.py:40
  286.7 18.7 %all_gather.15 = bf16[128,3584]{0,1:T(8,128)(2,1)S(1)} all-gather(bf16[128,224]{0,1:T(8,128)(2,1)S(1)} %copy-done.4), channel_id=1, replica_groups=mesh['grp'=16,'loc'=8] {'grp'}, dimensions={1}, use_global_device_ids=true | all-gather | bytes 974848 | tf_op jit(solution)/shard_map/all_gather | solution.py:41
  305.4 14.8 %reshape.82 = bf16[1152,3584]{1,0:T(8,128)(2,1)} reshape(bf16[128,9,3584]{2,1,0:T(8,128)(2,1)} %all-to-all-done) | data formatting | bytes 16515072 | tf_op jit(solution)/shard_map/reshape | solution.py:72
  320.2 5.3 fusion.37
  325.5 11.7 %convolution_convert_fusion.1 = bf16[1024,3584]{1,0:T(8,128)(2,1)} fusion(bf16[128,3584]{0,1:T(8,128)(2,1)S(1)} %all_gather.15, bf16[1024,3584]{1,0:T(8,128)(2,1)} %all-gather.2.cloned.1.call-done, bf16[3584,128]{1,0:T(8,128)(2,1)S(1)} %all_gather.14, f32[1024,128]{1,0:T(8,128)S(1)} %fusion.37), kind=kOutput, calls=%fused_computation.5 | convolution fusion | flops 1883504640 | bytes 17039360 | tf_op jit(solution)/shard_map/dot_general | solution.py:48
  337.2 12.3 %fusion.7 = f32[1152,1024]{1,0:T(8,128)S(1)} fusion(bf16[1152,3584]{1,0:T(8,128)(2,1)} %reshape.82, bf16[1,3584,1024]{2,1,0:T(8,128)(2,1)} %param.16), kind=kOutput, calls=%fused_computation.13 | convolution fusion | flops 8455716864 | bytes 20316160 | tf_op jit(solution)/shard_map/dot_general | solution.py:10
  349.6 13.6 %fusion.12 = bf16[1152,1024]{1,0:T(8,128)(2,1)S(1)} fusion(bf16[1152,3584]{1,0:T(8,128)(2,1)} %reshape.82, bf16[1,3584,1024]{2,1,0:T(8,128)(2,1)} %param.17, f32[1152,1024]{1,0:T(8,128)S(1)} %fusion.7), kind=kOutput, calls=%fused_computation.16 | convolution fusion | flops 8462794752 | bytes 22675456 | tf_op jit(solution)/shard_map/dot_general | solution.py:11
  363.2 13.7 %convolution_convert_fusion = bf16[1152,3584]{1,0:T(8,128)(2,1)} fusion(bf16[1152,1024]{1,0:T(8,128)(2,1)S(1)} %fusion.12, bf16[1,1024,3584]{2,1,0:T(8,128)(2,1)} %param.18), kind=kOutput, calls=%fused_computation.3 | convolution fusion | flops 8459845632 | bytes 17956864 | tf_op jit(solution)/shard_map/dot_general | solution.py:13
  376.9 14.3 %reshape.83 = bf16[128,9,3584]{2,1,0:T(8,128)(2,1)} reshape(bf16[1152,3584]{1,0:T(8,128)(2,1)} %convolution_convert_fusion) | data formatting | bytes 16515072 | tf_op jit(solution)/shard_map/reshape | solution.py:74
  391.2 34.2 %all-to-all-start.1 = ((bf16[128,9,3584]{2,1,0:T(8,128)(2,1)}), bf16[128,9,3584]{2,1,0:T(8,128)(2,1)}, u32[]{:S(2)}, u32[]{:S(2)}) async-start(bf16[128,9,3584]{2,1,0:T(8,128)(2,1)} %reshape.83), calls=%async_computation.2 | async-start | bytes 29360128 | tf_op jit(solution)/shard_map/all_to_all | solution.py:76
  425.5 0.1 copy.18
  425.6 192.8 %all-to-all-done.1 = bf16[128,9,3584]{2,1,0:T(8,128)(2,1)} async-done(((bf16[128,9,3584]{2,1,0:T(8,128)(2,1)}), bf16[128,9,3584]{2,1,0:T(8,128)(2,1)}, u32[]{:S(2)}, u32[]{:S(2)}) %all-to-all-start.1) | async-done | bytes 8257568 | tf_op jit(solution)/shard_map/all_to_all | solution.py:76
  618.4 14.6 %reshape.84 = bf16[1152,3584]{1,0:T(8,128)(2,1)} reshape(bf16[128,9,3584]{2,1,0:T(8,128)(2,1)} %all-to-all-done.1) | data formatting | bytes 16515072 | tf_op jit(solution)/shard_map/reshape | solution.py:77
  633.0 18.2 %gather_fusion.1 = bf16[1024,3584]{1,0:T(8,128)(2,1)} fusion(bf16[1152,3584]{1,0:T(8,128)(2,1)} %reshape.84, s32[1024]{0:T(1024)S(1)} %broadcast_clamp_fusion), kind=kCustom, calls=%fused_computation.1 | custom fusion | bytes 14684160 | tf_op jit(solution)/shard_map/gather | solution.py:77
  651.2 7.2 %fusion = f32[128,1,8]{2,1,0:T(1,128)S(1)} fusion(bf16[1024,3584]{1,0:T(8,128)(2,1)} %gather_fusion.1, bf16[128,3584,1]{1,0,2:T(8,128)(2,1)S(1)} %bitcast.44), kind=kOutput, calls=%fused_computation.6 | convolution fusion | flops 7340032 | bytes 8261632 | tf_op jit(solution)/shard_map/tkd,td->tk/dot_general | solution.py:81
  658.4 0.7 copy.21
  659.1 5.1 fusion.2
  664.2 2.3 fusion.18
  (35 shorter events, 0.8 us)
Async XLA Ops:
  7.2 644.0 %copy-start = (bf16[128,3584]{1,0:T(8,128)(2,1)S(1)}, bf16[128,3584]{1,0:T(8,128)(2,1)}, u32[]{:S(2)}) copy-start(bf16[128,3584]{1,0:T(8,128)(2,1)} %param.21) | copy-start | bytes 2752516
  7.2 313.0 %all-gather.2.cloned.1.call-start = ((), (), s32[]{:S(2)}) async-start(), calls=%async_computation.3 | async-start | bytes 8257536 | tf_op jit(solution)/shard_map/all_gather | solution.py:43
  11.1 7.2 %copy-start.1 = (bf16[128,3584]{1,0:T(8,128)(2,1)S(1)}, bf16[128,3584]{1,0:T(8,128)(2,1)}, u32[]{:S(2)}) copy-start(bf16[128,3584]{1,0:T(8,128)(2,1)} %fusion.17) | copy-start | bytes 2752516
  51.6 11.8 %copy-start.2 = (bf16[224,128]{1,0:T(8,128)(2,1)S(1)}, bf16[224,128]{1,0:T(8,128)(2,1)}, u32[]{:S(2)}) copy-start(bf16[224,128]{1,0:T(8,128)(2,1)} %param.13) | copy-start | bytes 172036
  51.6 218.1 %copy-start.3 = (bf16[224,128]{1,0:T(8,128)(2,1)S(1)}, bf16[224,128]{1,0:T(8,128)(2,1)}, u32[]{:S(2)}) copy-start(bf16[224,128]{1,0:T(8,128)(2,1)} %param.14) | copy-start | bytes 172036
  51.6 235.1 %copy-start.4 = (bf16[128,224]{0,1:T(8,128)(2,1)S(1)}, bf16[128,224]{0,1:T(8,128)(2,1)}, u32[]{:S(2)}) copy-start(bf16[128,224]{0,1:T(8,128)(2,1)} %param.15) | copy-start | bytes 172036
  51.6 253.8 %all-to-all-start = ((bf16[128,9,3584]{2,1,0:T(8,128)(2,1)}), bf16[128,9,3584]{2,1,0:T(8,128)(2,1)}, u32[]{:S(2)}, u32[]{:S(2)}) async-start(bf16[128,9,3584]{2,1,0:T(8,128)(2,1)} %broadcast_select_fusion), calls=%async_computation.1 | async-start | bytes 29360128 | tf_op jit(solution)/shard_map/all_to_all | solution.py:70
  63.3 600.9 %reduce-scatter.2.cloned.1.call-start = ((), (), s32[]{:S(2)}) async-start(), calls=%async_computation.4 | async-start | bytes 8257536 | tf_op jit(solution)/shard_map/reduce_scatter | solution.py:47
  391.2 34.2 %copy-start.5 = (bf16[128,8]{0,1:T(8,128)(2,1)S(1)}, bf16[128,8]{0,1:T(8,128)(2,1)}, u32[]{:S(2)}) copy-start(bf16[128,8]{0,1:T(8,128)(2,1)} %param.20) | copy-start | bytes 6148
  391.2 227.2 %all-to-all-start.1 = ((bf16[128,9,3584]{2,1,0:T(8,128)(2,1)}), bf16[128,9,3584]{2,1,0:T(8,128)(2,1)}, u32[]{:S(2)}, u32[]{:S(2)}) async-start(bf16[128,9,3584]{2,1,0:T(8,128)(2,1)} %reshape.83), calls=%async_computation.2 | async-start | bytes 29360128 | tf_op jit(solution)/shard_map/all_to_all | solution.py:76
Sparse Core Ops, SparseCore 0:
  11.3 49.1 all-gather.1
  337.4 72.1 reduce-scatter.1
where the time goes:
time: 686 us; the launch traced here: 673 us
  blocking collectives  242 us (35%)
  waiting for transfers between devices  193 us (28%)
  local copies, waits for them, and re-layouts  90.5 us (13%)
  matrix products  69 us (10%)
  starting transfers between devices  46 us (7%)
  other arithmetic  18.7 us (3%)
  between operations  14.2 us (2%)
    all_gather x1, blocking collectives, body(): lax.all_gather(shared_gate, 'grp', axis=0, tiled=True)  206 us
    all_to_all x1, waiting for transfers between devices, body(): lax.all_to_all(outcome, ('grp', 'loc'), split_axis=0, concat_axis=0, tile...  193 us
    all_to_all x1, starting transfers between devices, body(): lax.all_to_all(outcome, ('grp', 'loc'), split_axis=0, concat_axis=0, tile...  34.2 us
    gather x2, local copies, waits for them, and re-layouts, body(): normed[jnp.maximum(slot_token, 0)]  21.8 us
    all_gather x1, blocking collectives, body(): lax.all_gather(shared_down, 'grp', axis=1, tiled=True)  18.7 us
    gather x1, local copies, waits for them, and re-layouts, body(): returned.reshape(experts * slot_count, model_width)[slot_of_pair]  18.2 us
    all_gather x1, blocking collectives, body(): lax.all_gather(shared_up, 'grp', axis=0, tiled=True)  17 us
    reshape x1, local copies, waits for them, and re-layouts, body(): parcel.reshape(-1, model_width)  14.8 us
  transfers between devices with their start and end apart: 4, of which 1 were waited for; matrix products, arithmetic and copies ran while one was open for 23% of the time, Pallas kernels for 0%

commit v1 on v0

v1 whole, which is shorter than its diff:
```python
import functools

import jax
import jax.numpy as jnp
from jax import lax
from jax.experimental import pallas as pl
from jax.experimental.pallas import tpu as pltpu
from jax.sharding import PartitionSpec as P

MESH = pl.DeviceIdType.MESH
F32 = jnp.float32
BF16 = jnp.bfloat16
EPS = 1e-06

D = 3584
FF = 1024
SH = 128
T = 128
GRP, LOC = 16, 8
COL = LOC * T
CAP = 72
W = 512
HALF = W // 2
NS = D // W
PACK = 2 * CAP
SUP = 80
SHARD = D // GRP
ORDER = (
    (0, 1), (0, 3), (1, 0), (3, 0), (1, 1), (3, 3), (1, 3), (3, 1),
    (0, 2), (2, 0), (2, 1), (2, 3), (1, 2), (3, 2), (2, 2),
)
VMEM_LIMIT = 60 * 2**20


def place():
    g, l = lax.axis_index("grp"), lax.axis_index("loc")
    return g, l, l // 2, l % 2


def grp_partner(g, step):
    dy, dx = step
    return ((g // 4 + dy) % 4) * 4 + (g % 4 + dx) % 4


def loc_partner(z, c, dz, dc):
    pz, pc = (z + dz) % 4, (c + dc) % 2
    return pz * 2 + pc, pc * 4 + pz


LOC_STEPS = ((1, 0), (3, 0), (1, 1), (3, 1), (2, 0), (2, 1), (0, 1))


def send(src, dst, send_sem, recv_sem, device):
    copy = pltpu.make_async_remote_copy(
        src_ref=src,
        dst_ref=dst,
        send_sem=send_sem,
        recv_sem=recv_sem,
        device_id=device,
        device_id_type=MESH,
    )
    copy.start()


def drain(ref, sem):
    pltpu.make_async_copy(ref, ref, sem).wait()


def enter(g, l, z, c):
    barrier = pltpu.get_barrier_semaphore()
    for step in ORDER:
        pl.semaphore_signal(
            barrier, inc=1, device_id=(grp_partner(g, step), l), device_id_type=MESH
        )
    for dz, dc in LOC_STEPS:
        pl.semaphore_signal(
            barrier, inc=1, device_id=(g, loc_partner(z, c, dz, dc)[0]), device_id_type=MESH
        )
    return barrier


def dot(a, b):
    return jnp.dot(a, b, preferred_element_type=F32)


def dot_nt(a, b):
    return lax.dot_general(a, b, (((1,), (1,)), ((), ())), preferred_element_type=F32)


def silu(v):
    return v / (1.0 + jnp.exp(-v))


def dispatch_kernel(
    stream, gain, meta, sg, su, cot, wg, wu,
    hidden, shared_hidden, slots, gates, ids_all, cot_all,
    xall, onehot, sbuf, rbuf, accg, accu, wgb, wub, wsh, sacc, meta_all,
    ms, mr, ag_s, ag_r, sib_s, sib_r, cg_s, cg_r, cs_s, cs_r, c_l, d_s, d_r, d_l,
    w_s, w_r, w_l, hbm,
):
    g, l, z, c = place()
    me = c * 4 + z
    barrier = enter(g, l, z, c)
    sibling = loc_partner(z, c, 0, 1)[0]

    def weights(s, slot):
        rows = pl.ds(pl.multiple_of(s * W, W), W)
        return (
            pltpu.make_async_copy(wg.at[0, rows], wgb.at[slot], hbm.at[0, slot]),
            pltpu.make_async_copy(wu.at[0, rows], wub.at[slot], hbm.at[1, slot]),
        )

    for copy in weights(0, 0):
        copy.start()
    meta_all[me] = meta[...]

    def norm_rows(i, carry):
        rows = pl.ds(pl.multiple_of(i * 16, 16), 16)
        v = stream[rows, :].astype(F32)
        scale = lax.rsqrt(jnp.mean(v * v, axis=1, keepdims=True) + EPS)
        n = (v * scale * gain[...]).astype(BF16)
        for s in range(NS):
            xall[s, me, rows, :] = n[:, s * W : (s + 1) * W]
        return carry

    lax.fori_loop(0, T // 16, norm_rows, 0)

    pl.semaphore_wait(barrier, len(ORDER) + len(LOC_STEPS))

    for dz, dc in LOC_STEPS:
        send(meta_all.at[me], meta_all.at[me], ms, mr, (g, loc_partner(z, c, dz, dc)[0]))

    def gather(s, carry):
        for dz in (1, 3, 2):
            send(
                xall.at[s, me], xall.at[s, me], ag_s.at[s], ag_r.at[s],
                (g, loc_partner(z, c, dz, 0)[0]),
            )
        return carry

    lax.fori_loop(0, NS, gather, 0)
    own_rows = pl.ds(pl.multiple_of(g * SHARD, SHARD), SHARD)
    shard_copies = [
        pltpu.make_async_copy(sg, wsh.at[own_rows, 0:SH], w_l.at[0]),
        pltpu.make_async_copy(su, wsh.at[own_rows, SH : 2 * SH], w_l.at[1]),
    ]
    for copy in shard_copies:
        copy.start()

    accg[...] = jnp.zeros_like(accg)
    accu[...] = jnp.zeros_like(accu)
    sacc[...] = jnp.zeros_like(sacc)

    drain(meta_all.at[pl.ds(0, LOC - 1)], mr)
    ids = jnp.concatenate([meta_all[b, 0:8, :] for b in range(LOC)], axis=1)
    gws = jnp.concatenate([meta_all[b, 8:16, :] for b in range(LOC)], axis=1)
    ids_all[...] = ids
    expert = (lax.broadcasted_iota(jnp.int32, (GRP, COL), 0) * LOC + l).astype(F32)
    named = jnp.zeros((GRP, COL), F32)
    gate = jnp.zeros((GRP, COL), F32)
    for k in range(8):
        hit = ids[k : k + 1, :] == expert
        named = named + jnp.where(hit, 1.0, 0.0)
        gate = gate + jnp.where(hit, gws[k : k + 1, :], 0.0)
    before = jnp.where(
        lax.broadcasted_iota(jnp.int32, (T, T), 0) < lax.broadcasted_iota(jnp.int32, (T, T), 1),
        1.0,
        0.0,
    ).astype(BF16)
    ranks = [
        dot(named[:, b * T : (b + 1) * T].astype(BF16), before) + float(b * (CAP // LOC))
        for b in range(LOC)
    ]
    slot = jnp.where(named > 0.5, jnp.concatenate(ranks, axis=1), -100.0)
    slots[...] = slot
    gates[...] = gate
    row = lax.broadcasted_iota(jnp.int32, (CAP, COL), 0).astype(F32)
    for p in range(GRP // 2):
        pair = [jnp.where(row == slot[2 * p + i : 2 * p + i + 1, :], 1.0, 0.0) for i in (0, 1)]
        onehot[pl.ds(PACK * p, PACK), :] = jnp.concatenate(pair, axis=0).astype(BF16)

    def to_sibling(s):
        drain(xall.at[s, pl.ds(0, 3)], ag_r.at[s])
        mine = xall.at[s, pl.ds(c * 4, 4)]
        send(mine, mine, sib_s.at[s], sib_r.at[s], (g, sibling))

    def exchange(s):
        drain(xall.at[s, pl.ds(0, 4)], sib_r.at[s])

        def rows(i, carry):
            x = xall[s].reshape(COL, W)
            o = dot(onehot[pl.ds(pl.multiple_of(i * 4 * CAP, 4 * CAP), 4 * CAP), :], x)
            o = o.reshape(4, CAP, W)
            sbuf[s, pl.ds(i * 4, 4)] = jnp.concatenate(
                [o[:, :, :HALF], o[:, :, HALF:]], axis=1
            ).astype(BF16)
            return carry

        lax.fori_loop(0, GRP // 4, rows, 0)
        for step in ORDER:
            p = grp_partner(g, step)
            send(sbuf.at[s, p], rbuf.at[s, g], d_s.at[s], d_r.at[s], (p, l))
        pltpu.make_async_copy(sbuf.at[s, g], rbuf.at[s, g], d_l.at[s]).start()

    def cot_gather(s):
        cols = cot.at[:, pl.ds(pl.multiple_of(s * W, W), W)]
        pltpu.make_async_copy(cols, cot_all.at[s, me], c_l.at[s]).start()
        for dz in (1, 3, 2):
            send(
                cols, cot_all.at[s, me], cg_s.at[s], cg_r.at[s],
                (g, loc_partner(z, c, dz, 0)[0]),
            )

    def cot_sibling(s):
        drain(cot_all.at[s, pl.ds(0, 3)], cg_r.at[s])
        drain(cot_all.at[s, 0], c_l.at[s])
        mine = cot_all.at[s, pl.ds(c * 4, 4)]
        send(mine, mine, cs_s.at[s], cs_r.at[s], (g, sibling))

    def expert_in(s):
        slot_now = s % 2
        for copy in weights(s, slot_now):
            copy.wait()
        drain(rbuf.at[s, pl.ds(0, GRP - 1)], d_r.at[s])
        drain(rbuf.at[s, 0], d_l.at[s])

        def rows(i, carry):
            xa = rbuf[s, pl.ds(i * 4, 4), 0:SUP, :].reshape(4 * SUP, HALF)
            xb = rbuf[s, pl.ds(i * 4, 4), PACK - SUP : PACK, :].reshape(4 * SUP, HALF)
            for acc, w in ((accg, wgb), (accu, wub)):
                for n in range(2):
                    cols = slice(n * W, (n + 1) * W)
                    a = dot(xa, w[slot_now, 0:HALF, cols]).reshape(4, SUP, W)
                    b = dot(xb, w[slot_now, HALF:W, cols]).reshape(4, SUP, W)
                    acc[pl.ds(i * 4, 4), :, cols] += a[:, 0:CAP] + b[:, SUP - CAP :]
            return carry

        lax.fori_loop(0, GRP // 4, rows, 0)

    to_sibling(0)
    exchange(0)
    to_sibling(1)

    def step(s, carry):
        for copy in weights(s + 1, (s + 1) % 2):
            copy.start()
        exchange(s + 1)

        @pl.when(s + 2 < NS)
        def _():
            to_sibling(s + 2)

        cot_gather(s)

        @pl.when(s > 0)
        def _():
            cot_sibling(s - 1)

        expert_in(s)
        return carry

    def shard_sends(steps):
        for st in steps:
            p = grp_partner(g, st)
            send(sg, wsh.at[own_rows, 0:SH], w_s.at[0], w_r.at[0], (p, l))
            send(su, wsh.at[own_rows, SH : 2 * SH], w_s.at[1], w_r.at[1], (p, l))

    lax.fori_loop(0, 2, step, 0)
    shard_sends(ORDER)
    lax.fori_loop(2, NS - 1, step, 0)
    cot_gather(NS - 1)
    cot_sibling(NS - 2)

    for copy in shard_copies:
        copy.wait()
    drain(wsh.at[pl.ds(0, D - SHARD), 0:SH], w_r.at[0])
    drain(wsh.at[pl.ds(0, D - SHARD), SH : 2 * SH], w_r.at[1])

    def shared_in(s, carry):
        w = wsh[pl.ds(pl.multiple_of(s * W, W), W), :]
        for i in range(2):
            x = xall[s, pl.ds(i * 4, 4)].reshape(COL // 2, W)
            sacc[pl.ds(i * COL // 2, COL // 2), :] += dot(x, w)
        return carry

    lax.fori_loop(0, NS, shared_in, 0)
    shared_hidden[...] = (silu(sacc[:, 0:SH]) * sacc[:, SH : 2 * SH]).astype(BF16)

    cot_sibling(NS - 1)
    expert_in(NS - 1)

    def activate(i, carry):
        h = silu(accg[pl.ds(i * 2, 2)]) * accu[pl.ds(i * 2, 2)]
        hidden[pl.ds(pl.multiple_of(i * PACK, PACK), PACK), :] = h.reshape(PACK, FF).astype(BF16)
        return carry

    lax.fori_loop(0, GRP // 2, activate, 0)

    drain(meta_all.at[pl.ds(0, LOC - 1)], ms)
    drain(wsh.at[pl.ds(0, D - SHARD), 0:SH], w_s.at[0])
    drain(wsh.at[pl.ds(0, D - SHARD), SH : 2 * SH], w_s.at[1])

    def finish(s, carry):
        drain(xall.at[s, pl.ds(0, 3)], ag_s.at[s])
        drain(xall.at[s, pl.ds(0, 4)], sib_s.at[s])
        drain(cot_all.at[s, pl.ds(0, 3)], cg_s.at[s])
        drain(cot_all.at[s, pl.ds(0, 4)], cs_s.at[s])
        drain(cot_all.at[s, pl.ds(0, 4)], cs_r.at[s])
        drain(sbuf.at[s, pl.ds(0, GRP - 1)], d_s.at[s])
        return carry

    lax.fori_loop(0, NS, finish, 0)


def return_kernel(
    hidden, shared_hidden, slots, gates, ids_all, sd, cot_all, wd,
    out, gg,
    cwa, cwb, ohw, slots4, gacc, wdb, cotb, osend, orecv, psend, rrecv, sda, ggs, ggr,
    o_s, o_r, o_l, p_s, p_r, w_s, w_r, w_l, g_s, g_r, hbm, cot_sem,
):
    g, l, z, c = place()
    me = c * 4 + z
    barrier = enter(g, l, z, c)

    def weights(s, slot):
        cols = pl.ds(pl.multiple_of(s * W, W), W)
        return pltpu.make_async_copy(wd.at[0, :, cols], wdb.at[slot], hbm.at[slot])

    def cotangents(s, slot):
        return pltpu.make_async_copy(cot_all.at[s], cotb.at[slot], cot_sem.at[slot])

    weights(0, 0).start()
    weights(1, 1).start()
    cotangents(0, 0).start()
    own_rows = pl.ds(pl.multiple_of(g * SHARD, SHARD), SHARD)
    own_shard = pltpu.make_async_copy(sd, sda.at[own_rows], w_l)
    own_shard.start()

    def expert_out(s):
        slot_now = s % 2
        weights(s, slot_now).wait()

        def rows(i, carry):
            h = hidden[pl.ds(pl.multiple_of(i * 4 * CAP, 4 * CAP), 4 * CAP), :]
            o = dot(h, wdb[slot_now]).reshape(4, CAP, W)
            osend[s, pl.ds(i * 4, 4)] = jnp.concatenate(
                [o[:, :, :HALF], o[:, :, HALF:]], axis=1
            ).astype(BF16)
            return carry

        lax.fori_loop(0, GRP // 4, rows, 0)
        for step in ORDER:
            p = grp_partner(g, step)
            send(osend.at[s, p], orecv.at[s, g], o_s.at[s], o_r.at[s], (p, l))
        pltpu.make_async_copy(osend.at[s, g], orecv.at[s, g], o_l.at[s]).start()

    pl.semaphore_wait(barrier, len(ORDER) + len(LOC_STEPS))
    for step in ORDER:
        send(sd, sda.at[own_rows], w_s, w_r, (grp_partner(g, step), l))
    expert_out(0)

    slot = slots[...]
    gate = gates[...]
    for i in range(4):
        slots4[i] = slot[4 * i : 4 * i + 4, :]
    gacc[...] = jnp.zeros_like(gacc)
    row = lax.broadcasted_iota(jnp.int32, (SUP, COL), 0).astype(F32)
    for cw, shift in ((cwa, 0.0), (cwb, float(SUP - CAP))):
        for e in range(GRP):
            hit = (row - shift) == slot[e : e + 1, :]
            ohw[pl.ds(SUP * e, SUP), :] = jnp.where(hit, gate[e : e + 1, :], 0.0).astype(BF16)
        for j in range(GRP * SUP // T):
            block = ohw[pl.ds(T * j, T), :].astype(F32)
            cw[:, pl.ds(T * j, T)] = block.T.astype(BF16)

    expert_out(1)
    own_shard.wait()
    drain(sda.at[pl.ds(0, D - SHARD)], w_r)

    def combine(s):
        slot_now = s % 2
        drain(orecv.at[s, pl.ds(0, GRP - 1)], o_r.at[s])
        drain(orecv.at[s, 0], o_l.at[s])
        for half in range(2):
            first = 0 if half == 0 else PACK - SUP
            cw = cwa if half == 0 else cwb
            rows_sd = pl.ds(pl.multiple_of(s * W + half * HALF, HALF), HALF)
            cols = slice(half * HALF, (half + 1) * HALF)

            def tokens(i, carry):
                y = orecv[s, :, first : first + SUP, :].reshape(GRP * SUP, HALF)
                rows = pl.ds(pl.multiple_of(i * 256, 256), 256)
                part = dot(cw[rows, :], y) + dot_nt(shared_hidden[rows, :], sda[rows_sd, :])
                psend[s, pl.ds(i * 2, 2), :, cols] = part.reshape(2, T, HALF).astype(BF16)
                return carry

            lax.fori_loop(0, COL // 256, tokens, 0)
        for dz, dc in LOC_STEPS:
            pl_, blk = loc_partner(z, c, dz, dc)
            send(psend.at[s, blk], rrecv.at[s, me], p_s.at[s], p_r.at[s], (g, pl_))
        rrecv[s, me] = psend[s, me]

        cotangents(s, slot_now).wait()
        for half in range(2):
            first = 0 if half == 0 else PACK - SUP
            shift = 0.0 if half == 0 else float(SUP - CAP)
            cols = slice(half * HALF, (half + 1) * HALF)

            def products(i, carry):
                y = orecv[s, pl.ds(i * 4, 4), first : first + SUP, :].reshape(4 * SUP, HALF)
                pos = lax.broadcasted_iota(jnp.int32, (SUP, COL // 2), 0).astype(F32) - shift
                for h in range(2):
                    tok = slice(h * COL // 2, (h + 1) * COL // 2)
                    ct = cotb[slot_now, pl.ds(h * 4, 4), :, cols].reshape(COL // 2, HALF)
                    prod = dot_nt(y, ct).reshape(4, SUP, COL // 2)
                    sl = slots4[i, :, tok]
                    sums = [
                        jnp.sum(
                            jnp.where(pos == sl[e : e + 1, :], prod[e], 0.0), axis=0, keepdims=True
                        )
                        for e in range(4)
                    ]
                    gacc[i, :, tok] += jnp.concatenate(sums, axis=0)
                return carry

            lax.fori_loop(0, GRP // 4, products, 0)

    def total(s):
        drain(rrecv.at[s, pl.ds(0, LOC - 1)], p_r.at[s])
        acc = rrecv[s, 0].astype(F32)
        for b in range(1, LOC):
            acc = acc + rrecv[s, b].astype(F32)
        out[:, pl.ds(pl.multiple_of(s * W, W), W)] = acc.astype(BF16)

    def step(s, carry):
        @pl.when(s + 1 < NS)
        def _():
            cotangents(s + 1, (s + 1) % 2).start()

        @pl.when(s + 2 < NS)
        def _():
            weights(s + 2, s % 2).start()

        combine(s)

        @pl.when(s + 2 < NS)
        def _():
            expert_out(s + 2)

        @pl.when(s > 0)
        def _():
            total(s - 1)

        return carry

    lax.fori_loop(0, NS, step, 0)

    ids = ids_all[...]
    grads = jnp.zeros((8, COL), F32)
    for i in range(4):
        block = gacc[i]
        for j in range(4):
            e = ((4 * i + j) * LOC + l).astype(F32)
            grads = grads + jnp.where(ids == e, block[j : j + 1, :], 0.0)
    for b in range(LOC):
        ggs[b] = grads[:, b * T : (b + 1) * T]
    for dz, dc in LOC_STEPS:
        pl_, blk = loc_partner(z, c, dz, dc)
        send(ggs.at[blk], ggr.at[me], g_s, g_r, (g, pl_))
    ggr[me] = ggs[me]
    total(NS - 1)
    drain(ggr.at[pl.ds(0, LOC - 1)], g_r)
    acc = ggr[0]
    for b in range(1, LOC):
        acc = acc + ggr[b]
    gg[...] = acc

    drain(ggs.at[pl.ds(0, LOC - 1)], g_s)
    drain(sda.at[pl.ds(0, D - SHARD)], w_s)

    def finish(s, carry):
        drain(osend.at[s, pl.ds(0, GRP - 1)], o_s.at[s])
        drain(psend.at[s, pl.ds(0, LOC - 1)], p_s.at[s])
        return carry

    lax.fori_loop(0, NS, finish, 0)


def body(
    stream_in, norm_gain, shared_gate, shared_up, shared_down, expert_gate, expert_up, expert_down,
    expert_ids, gate_weights, cotangent,
):
    vm = pl.BlockSpec(memory_space=pltpu.VMEM)
    hb = pl.BlockSpec(memory_space=pl.ANY)
    dma = pltpu.SemaphoreType.DMA
    meta = jnp.concatenate([expert_ids.T.astype(F32), gate_weights.T.astype(F32)], axis=0)
    hidden, shared_hidden, slots, gates, ids_all, cot_all = pl.pallas_call(
        dispatch_kernel,
        out_shape=(
            jax.ShapeDtypeStruct((GRP * CAP, FF), BF16),
            jax.ShapeDtypeStruct((COL, SH), BF16),
            jax.ShapeDtypeStruct((GRP, COL), F32),
            jax.ShapeDtypeStruct((GRP, COL), F32),
            jax.ShapeDtypeStruct((8, COL), F32),
            jax.ShapeDtypeStruct((NS, LOC, T, W), BF16),
        ),
        in_specs=[vm] * 6 + [hb] * 2,
        out_specs=(vm,) * 5 + (hb,),
        scratch_shapes=[
            pltpu.VMEM((NS, LOC, T, W), BF16),
            pltpu.VMEM((GRP * CAP, COL), BF16),
            pltpu.VMEM((NS, GRP, PACK, HALF), BF16),
            pltpu.VMEM((NS, GRP, PACK, HALF), BF16),
            pltpu.VMEM((GRP, CAP, FF), F32),
            pltpu.VMEM((GRP, CAP, FF), F32),
            pltpu.VMEM((2, W, FF), BF16),
            pltpu.VMEM((2, W, FF), BF16),
            pltpu.VMEM((D, 2 * SH), BF16),
            pltpu.VMEM((COL, 2 * SH), F32),
            pltpu.VMEM((LOC, 16, T), F32),
        ]
        + [dma(()), dma(())]
        + [dma((NS,))] * 12
        + [dma((2,))] * 3
        + [dma((2, 2))],
        compiler_params=pltpu.CompilerParams(
            collective_id=0, has_side_effects=True, vmem_limit_bytes=VMEM_LIMIT
        ),
        name="dispatch",
    )(
        stream_in, norm_gain.reshape(1, D), meta, shared_gate, shared_up, cotangent,
        expert_gate, expert_up,
    )
    out, grads = pl.pallas_call(
        return_kernel,
        out_shape=(
            jax.ShapeDtypeStruct((T, D), BF16),
            jax.ShapeDtypeStruct((8, T), F32),
        ),
        in_specs=[vm] * 6 + [hb] * 2,
        out_specs=(vm, vm),
        scratch_shapes=[
            pltpu.VMEM((COL, GRP * SUP), BF16),
            pltpu.VMEM((COL, GRP * SUP), BF16),
            pltpu.VMEM((GRP * SUP, COL), BF16),
            pltpu.VMEM((4, 4, COL), F32),
            pltpu.VMEM((4, 4, COL), F32),
            pltpu.VMEM((2, FF, W), BF16),
            pltpu.VMEM((2, LOC, T, W), BF16),
            pltpu.VMEM((NS, GRP, PACK, HALF), BF16),
            pltpu.VMEM((NS, GRP, PACK, HALF), BF16),
            pltpu.VMEM((NS, LOC, T, W), BF16),
            pltpu.VMEM((NS, LOC, T, W), BF16),
            pltpu.VMEM((D, SH), BF16),
            pltpu.VMEM((LOC, 8, T), F32),
            pltpu.VMEM((LOC, 8, T), F32),
        ]
        + [dma((NS,))] * 5
        + [dma(())] * 5
        + [dma((2,))] * 2,
        compiler_params=pltpu.CompilerParams(
            collective_id=1, has_side_effects=True, vmem_limit_bytes=VMEM_LIMIT
        ),
        name="give_back",
    )(hidden, shared_hidden, slots, gates, ids_all, shared_down.T, cot_all, expert_down)
    return out, grads.T


def solution(mesh):
    rows = P(("grp", "loc"), None)
    experts = P(("grp", "loc"), None, None)
    return jax.shard_map(
        body,
        mesh=mesh,
        in_specs=(
            rows, P(), P("grp", "loc"), P("grp", "loc"), P("loc", "grp"), experts, experts, experts,
            rows, rows, rows,
        ),
        out_specs=(rows, rows),
        check_vma=False,
    )
```

time: 686 us -> 284 us (0.41); the launches traced: 673 us -> 281 us
  Pallas kernels: 0 us -> 274 us
  blocking collectives: 242 us -> 0 us
  waiting for transfers between devices: 193 us -> 0 us
  local copies, waits for them, and re-layouts: 90.5 us -> 4.75 us
  matrix products: 69 us -> 0 us
  starting transfers between devices: 46 us -> 0 us
  other arithmetic: 18.7 us -> 1.97 us
  between operations: 14.2 us -> 0.65 us
    pallas_call x0 -> x2, Pallas kernels: none -> 274 us  [the longest x1 141 us: body(): pl.pallas_call(dispatch_kernel, out_shape=(jax.ShapeDtypeStruct((GRP * CA...]
    all_gather x3 -> x0, blocking collectives: 242 us -> none  [the longest x1 206 us: body(): lax.all_gather(shared_gate, 'grp', axis=0, tiled=True)]
    all_to_all x2 -> x0, waiting for transfers between devices: 193 us -> none  [the longest x1 193 us: body(): lax.all_to_all(outcome, ('grp', 'loc'), split_axis=0, concat_axis=0, tile...]
    dot_general x7 -> x0, matrix products: 69 us -> none  [the longest x1 13.7 us: swiglu_rows(): return jnp.dot(hidden, w_down, preferred_element_type=jnp.float32)]
    all_to_all x2 -> x0, starting transfers between devices: 46 us -> none  [the longest x1 34.2 us: body(): lax.all_to_all(outcome, ('grp', 'loc'), split_axis=0, concat_axis=0, tile...]
    reshape x3 -> x1, local copies, waits for them, and re-layouts: 43.6 us -> 1.33 us  [body(): norm_gain.reshape(1, D)]
    gather x3 -> x0, local copies, waits for them, and re-layouts: 40 us -> none  [the longest x2 21.8 us: body(): normed[jnp.maximum(slot_token, 0)]]
    select_n x3 -> x0, other arithmetic: 11.1 us -> none  [the longest x1 11.1 us: body(): jnp.where(slot_filled[:, None], normed[jnp.maximum(slot_token, 0)], bf_zero)]
  transfers between devices with their start and end apart: 4 -> 0, of which waited for: 1 -> 0; matrix products, arithmetic and copies ran while one was open for 23% -> 0% of each run, Pallas kernels for 0% -> 0%
where the time goes in v1:
time: 284 us; the launch traced here: 281 us
  Pallas kernels  274 us (96%)
  local copies, waits for them, and re-layouts  4.75 us (2%)
    pallas_call x1, Pallas kernels, body(): pl.pallas_call(dispatch_kernel, out_shape=(jax.ShapeDtypeStruct((GRP * CA...  141 us
    pallas_call x1, Pallas kernels, body(): pl.pallas_call(return_kernel, out_shape=(jax.ShapeDtypeStruct((T, D), BF1...  133 us

profile of v1, /device:TPU:1, one launch (start us, length us, event | category | flops | bytes accessed | tf_op | source)
XLA Modules:
  0.0 281.2 jit_solution(4035622133790230011)
XLA Ops:
  0.6 0.7 convert_bitcast_fusion.1
  1.3 0.7 convert_bitcast_fusion
  2.0 0.6 pad_maximum_fusion.meta
  2.6 1.3 reshape.7.gain
  3.9 140.6 %dispatch.1 = (bf16[1152,1024]{1,0:T(8,128)(2,1)}, bf16[1024,128]{1,0:T(8,128)(2,1)}, f32[16,1024]{1,0:T(8,128)}, f32[16,1024]{1,0:T(8,128)}, f32[8,1024]{1,0:T(8,128)}, /*index=5*/bf16[7,8,128,512]{3,2,1,0:T(8,128)(2,1)}) custom-call(bf16[128,3584]{1,0:T(8,128)(2,1)} %stream.1, f32[1,3584]{1,0:T(1,128)} %reshape.7.gain, f32[16,128]{1,0:T(8,128)} %pad_maximum_fusion.meta, ...), custom_call_target="tpu_custom_call" | custom-call | tf_op jit(solution)/shard_map/dispatch/pallas_call | solution.py:497
  144.5 133.3 %give_back.1 = (bf16[128,3584]{1,0:T(8,128)(2,1)}, f32[8,128]{1,0:T(8,128)}) custom-call(bf16[1152,1024]{1,0:T(8,128)(2,1)} %get-tuple-element.10.hidden, bf16[1024,128]{1,0:T(8,128)(2,1)} %get-tuple-element.11.shared_hidden, f32[16,1024]{1,0:T(8,128)} %get-tuple-element.12.slots, f32[16,1024]{1,0:T(8,128)} %get-tuple-element.13.gates, ...), custom_call_target="tpu_custom_call" | custom-call | tf_op jit(solution)/shard_map/give_back/pallas_call | solution.py:534
  277.8 2.2 copy.15
  280.0 1.3 copy.16

commit v2 on v1

--- a/solution.py
+++ b/solution.py
@@ -92,8 +92,8 @@
 
 
 def dispatch_kernel(
-    stream, gain, meta, sg, su, cot, wg, wu,
-    hidden, shared_hidden, slots, gates, ids_all, cot_all,
+    stream, gain, ids_in, gw_in, sg, su, sd, cot, wg, wu,
+    hidden, shared_hidden, slots, gates, ids_all, cot_all, sd_all,
     xall, onehot, sbuf, rbuf, accg, accu, wgb, wub, wsh, sacc, meta_all,
     ms, mr, ag_s, ag_r, sib_s, sib_r, cg_s, cg_r, cs_s, cs_r, c_l, d_s, d_r, d_l,
     w_s, w_r, w_l, hbm,
@@ -112,13 +112,15 @@
 
     for copy in weights(0, 0):
         copy.start()
-    meta_all[me] = meta[...]
+    meta_all[me, 0:8, :] = ids_in[...].astype(F32)
+    meta_all[me, 8:16, :] = gw_in[...].astype(F32)
+    row_gain = gain[...].reshape(1, D)
 
     def norm_rows(i, carry):
         rows = pl.ds(pl.multiple_of(i * 16, 16), 16)
         v = stream[rows, :].astype(F32)
         scale = lax.rsqrt(jnp.mean(v * v, axis=1, keepdims=True) + EPS)
-        n = (v * scale * gain[...]).astype(BF16)
+        n = (v * scale * row_gain).astype(BF16)
         for s in range(NS):
             xall[s, me, rows, :] = n[:, s * W : (s + 1) * W]
         return carry
@@ -143,9 +145,14 @@
     shard_copies = [
         pltpu.make_async_copy(sg, wsh.at[own_rows, 0:SH], w_l.at[0]),
         pltpu.make_async_copy(su, wsh.at[own_rows, SH : 2 * SH], w_l.at[1]),
+        pltpu.make_async_copy(sd, sd_all.at[own_rows], w_l.at[2]),
     ]
     for copy in shard_copies:
         copy.start()
+    for st in ORDER:
+        p = grp_partner(g, st)
+        send(sg, wsh.at[own_rows, 0:SH], w_s.at[0], w_r.at[0], (p, l))
+        send(su, wsh.at[own_rows, SH : 2 * SH], w_s.at[1], w_r.at[1], (p, l))
 
     accg[...] = jnp.zeros_like(accg)
     accu[...] = jnp.zeros_like(accu)
@@ -259,15 +266,9 @@
         expert_in(s)
         return carry
 
-    def shard_sends(steps):
-        for st in steps:
-            p = grp_partner(g, st)
-            send(sg, wsh.at[own_rows, 0:SH], w_s.at[0], w_r.at[0], (p, l))
-            send(su, wsh.at[own_rows, SH : 2 * SH], w_s.at[1], w_r.at[1], (p, l))
-
-    lax.fori_loop(0, 2, step, 0)
-    shard_sends(ORDER)
-    lax.fori_loop(2, NS - 1, step, 0)
+    lax.fori_loop(0, NS - 1, step, 0)
+    for st in ORDER:
+        send(sd, sd_all.at[own_rows], w_s.at[2], w_r.at[2], (grp_partner(g, st), l))
     cot_gather(NS - 1)
     cot_sibling(NS - 2)
 
@@ -299,6 +300,8 @@
     drain(meta_all.at[pl.ds(0, LOC - 1)], ms)
     drain(wsh.at[pl.ds(0, D - SHARD), 0:SH], w_s.at[0])
     drain(wsh.at[pl.ds(0, D - SHARD), SH : 2 * SH], w_s.at[1])
+    drain(sd_all.at[pl.ds(0, D - SHARD)], w_s.at[2])
+    drain(sd_all.at[pl.ds(0, D - SHARD)], w_r.at[2])
 
     def finish(s, carry):
         drain(xall.at[s, pl.ds(0, 3)], ag_s.at[s])
@@ -313,10 +316,10 @@
 
 
 def return_kernel(
-    hidden, shared_hidden, slots, gates, ids_all, sd, cot_all, wd,
+    hidden, shared_hidden, slots, gates, ids_all, cot_all, sd_all, wd,
     out, gg,
     cwa, cwb, ohw, slots4, gacc, wdb, cotb, osend, orecv, psend, rrecv, sda, ggs, ggr,
-    o_s, o_r, o_l, p_s, p_r, w_s, w_r, w_l, g_s, g_r, hbm, cot_sem,
+    o_s, o_r, o_l, p_s, p_r, w_l, g_s, g_r, hbm, cot_sem,
 ):
     g, l, z, c = place()
     me = c * 4 + z
@@ -332,9 +335,8 @@
     weights(0, 0).start()
     weights(1, 1).start()
     cotangents(0, 0).start()
-    own_rows = pl.ds(pl.multiple_of(g * SHARD, SHARD), SHARD)
-    own_shard = pltpu.make_async_copy(sd, sda.at[own_rows], w_l)
-    own_shard.start()
+    shared_down = pltpu.make_async_copy(sd_all, sda, w_l)
+    shared_down.start()
 
     def expert_out(s):
         slot_now = s % 2
@@ -355,8 +357,6 @@
         pltpu.make_async_copy(osend.at[s, g], orecv.at[s, g], o_l.at[s]).start()
 
     pl.semaphore_wait(barrier, len(ORDER) + len(LOC_STEPS))
-    for step in ORDER:
-        send(sd, sda.at[own_rows], w_s, w_r, (grp_partner(g, step), l))
     expert_out(0)
 
     slot = slots[...]
@@ -374,8 +374,7 @@
             cw[:, pl.ds(T * j, T)] = block.T.astype(BF16)
 
     expert_out(1)
-    own_shard.wait()
-    drain(sda.at[pl.ds(0, D - SHARD)], w_r)
+    shared_down.wait()
 
     def combine(s):
         slot_now = s % 2
@@ -395,9 +394,12 @@
                 return carry
 
             lax.fori_loop(0, COL // 256, tokens, 0)
-        for dz, dc in LOC_STEPS:
-            pl_, blk = loc_partner(z, c, dz, dc)
-            send(psend.at[s, blk], rrecv.at[s, me], p_s.at[s], p_r.at[s], (g, pl_))
+            for dz, dc in LOC_STEPS:
+                pl_, blk = loc_partner(z, c, dz, dc)
+                send(
+                    psend.at[s, blk, :, cols], rrecv.at[s, me, :, cols], p_s.at[s], p_r.at[s],
+                    (g, pl_),
+                )
         rrecv[s, me] = psend[s, me]
 
         cotangents(s, slot_now).wait()
@@ -476,7 +478,6 @@
     gg[...] = acc
 
     drain(ggs.at[pl.ds(0, LOC - 1)], g_s)
-    drain(sda.at[pl.ds(0, D - SHARD)], w_s)
 
     def finish(s, carry):
         drain(osend.at[s, pl.ds(0, GRP - 1)], o_s.at[s])
@@ -493,8 +494,7 @@
     vm = pl.BlockSpec(memory_space=pltpu.VMEM)
     hb = pl.BlockSpec(memory_space=pl.ANY)
     dma = pltpu.SemaphoreType.DMA
-    meta = jnp.concatenate([expert_ids.T.astype(F32), gate_weights.T.astype(F32)], axis=0)
-    hidden, shared_hidden, slots, gates, ids_all, cot_all = pl.pallas_call(
+    hidden, shared_hidden, slots, gates, ids_all, cot_all, sd_all = pl.pallas_call(
         dispatch_kernel,
         out_shape=(
             jax.ShapeDtypeStruct((GRP * CAP, FF), BF16),
@@ -503,9 +503,10 @@
             jax.ShapeDtypeStruct((GRP, COL), F32),
             jax.ShapeDtypeStruct((8, COL), F32),
             jax.ShapeDtypeStruct((NS, LOC, T, W), BF16),
+            jax.ShapeDtypeStruct((D, SH), BF16),
         ),
-        in_specs=[vm] * 6 + [hb] * 2,
-        out_specs=(vm,) * 5 + (hb,),
+        in_specs=[vm] * 8 + [hb] * 2,
+        out_specs=(vm,) * 5 + (hb,) * 2,
         scratch_shapes=[
             pltpu.VMEM((NS, LOC, T, W), BF16),
             pltpu.VMEM((GRP * CAP, COL), BF16),
@@ -521,15 +522,15 @@
         ]
         + [dma(()), dma(())]
         + [dma((NS,))] * 12
-        + [dma((2,))] * 3
+        + [dma((3,))] * 3
         + [dma((2, 2))],
         compiler_params=pltpu.CompilerParams(
             collective_id=0, has_side_effects=True, vmem_limit_bytes=VMEM_LIMIT
         ),
         name="dispatch",
     )(
-        stream_in, norm_gain.reshape(1, D), meta, shared_gate, shared_up, cotangent,
-        expert_gate, expert_up,
+        stream_in, norm_gain, expert_ids.T, gate_weights.T, shared_gate, shared_up, shared_down.T,
+        cotangent, expert_gate, expert_up,
     )
     out, grads = pl.pallas_call(
         return_kernel,
@@ -537,7 +538,7 @@
             jax.ShapeDtypeStruct((T, D), BF16),
             jax.ShapeDtypeStruct((8, T), F32),
         ),
-        in_specs=[vm] * 6 + [hb] * 2,
+        in_specs=[vm] * 5 + [hb] * 3,
         out_specs=(vm, vm),
         scratch_shapes=[
             pltpu.VMEM((COL, GRP * SUP), BF16),
@@ -556,13 +557,13 @@
             pltpu.VMEM((LOC, 8, T), F32),
         ]
         + [dma((NS,))] * 5
-        + [dma(())] * 5
+        + [dma(())] * 3
         + [dma((2,))] * 2,
         compiler_params=pltpu.CompilerParams(
             collective_id=1, has_side_effects=True, vmem_limit_bytes=VMEM_LIMIT
         ),
         name="give_back",
-    )(hidden, shared_hidden, slots, gates, ids_all, shared_down.T, cot_all, expert_down)
+    )(hidden, shared_hidden, slots, gates, ids_all, cot_all, sd_all, expert_down)
     return out, grads.T
 
 

time: 284 us -> 262 us (0.923)
  Pallas kernels: 274 us -> 253 us
    pallas_call x1, Pallas kernels: 133 us -> 116 us  [body(): pl.pallas_call(return_kernel, out_shape=(jax.ShapeDtypeStruct((T, D), BF1...]
    pallas_call x1, Pallas kernels: 141 us -> 137 us  [body(): pl.pallas_call(dispatch_kernel, out_shape=(jax.ShapeDtypeStruct((GRP * CA...]
where the time goes in v2:
time: 262 us; the launch traced here: 257 us
  Pallas kernels  253 us (97%)
  local copies, waits for them, and re-layouts  3.43 us (1%)
    pallas_call x1, Pallas kernels, body(): pl.pallas_call(dispatch_kernel, out_shape=(jax.ShapeDtypeStruct((GRP * CA...  137 us
    pallas_call x1, Pallas kernels, body(): pl.pallas_call(return_kernel, out_shape=(jax.ShapeDtypeStruct((T, D), BF1...  116 us

profile of v2, /device:TPU:1, one launch (start us, length us, event | category | flops | bytes accessed | tf_op | source)
XLA Modules:
  0.0 257.2 jit_solution(1985481257173387444)
XLA Ops:
  0.6 136.8 %dispatch.1 = (bf16[1152,1024]{1,0:T(8,128)(2,1)}, bf16[1024,128]{1,0:T(8,128)(2,1)}, f32[16,1024]{1,0:T(8,128)}, f32[16,1024]{1,0:T(8,128)}, f32[8,1024]{1,0:T(...) custom-call(bf16[128,3584]{1,0:T(8,128)(2,1)} %stream.1, f32[3584]{0:T(1024)} %gain.1, ...), custom_call_target="tpu_custom_call" | custom-call | tf_op jit(solution)/shard_map/dispatch/pallas_call | solution.py:497
  137.5 116.3 %give_back.1 = (bf16[128,3584]{1,0:T(8,128)(2,1)}, f32[8,128]{1,0:T(8,128)}) custom-call(bf16[1152,1024]{1,0:T(8,128)(2,1)} %get-tuple-element.11.hidden, bf16[1024,128]{1,0:T(8,128)(2,1)} %get-tuple-element.12.shared_hidden, f32[16,1024]{1,0:T(8,128)} %get-tuple-element.13.slots, f32[16,1024]{1,0:T(8,128)} %get-tuple-element.14.gates, ...), custom_call_target="tpu_custom_call" | custom-call | tf_op jit(solution)/shard_map/give_back/pallas_call | solution.py:535
  253.8 2.2 copy.15
  256.0 1.3 copy.16

commit v3 on v2

--- a/solution.py
+++ b/solution.py
@@ -29,7 +29,8 @@
     (0, 1), (0, 3), (1, 0), (3, 0), (1, 1), (3, 3), (1, 3), (3, 1),
     (0, 2), (2, 0), (2, 1), (2, 3), (1, 2), (3, 2), (2, 2),
 )
-VMEM_LIMIT = 60 * 2**20
+RING = 4
+VMEM_LIMIT = 62 * 2**20
 
 
 def place():
@@ -91,11 +92,14 @@
     return v / (1.0 + jnp.exp(-v))
 
 
-def dispatch_kernel(
-    stream, gain, ids_in, gw_in, sg, su, sd, cot, wg, wu,
-    hidden, shared_hidden, slots, gates, ids_all, cot_all, sd_all,
+def layer_kernel(
+    stream, gain, ids_in, gw_in, sg, su, sd, cot, wg, wu, wd,
+    out, gg, cot_all,
     xall, onehot, sbuf, rbuf, accg, accu, wgb, wub, wsh, sacc, meta_all,
-    ms, mr, ag_s, ag_r, sib_s, sib_r, cg_s, cg_r, cs_s, cs_r, c_l, d_s, d_r, d_l,
+    hidden, shared_hidden, slots, gates, sda, cwa, cwb, slots4, gacc, rrecv, ggs, ggr,
+    ms, mr, g_s, g_r, free,
+    ag_s, ag_r, sib_s, sib_r, cg_s, cg_r, cs_s, cs_r, c_l, d_s, d_r, d_l,
+    o_s, o_r, o_l, p_s, p_r,
     w_s, w_r, w_l, hbm,
 ):
     g, l, z, c = place()
@@ -145,14 +149,14 @@
     shard_copies = [
         pltpu.make_async_copy(sg, wsh.at[own_rows, 0:SH], w_l.at[0]),
         pltpu.make_async_copy(su, wsh.at[own_rows, SH : 2 * SH], w_l.at[1]),
-        pltpu.make_async_copy(sd, sd_all.at[own_rows], w_l.at[2]),
+        pltpu.make_async_copy(sd, sda.at[own_rows], w_l.at[2]),
     ]
     for copy in shard_copies:
         copy.start()
-    for st in ORDER:
-        p = grp_partner(g, st)
-        send(sg, wsh.at[own_rows, 0:SH], w_s.at[0], w_r.at[0], (p, l))
-        send(su, wsh.at[own_rows, SH : 2 * SH], w_s.at[1], w_r.at[1], (p, l))
+    for d in (1, 3, 2):
+        along_x, along_y = (grp_partner(g, (0, d)), l), (grp_partner(g, (d, 0)), l)
+        send(sg, wsh.at[own_rows, 0:SH], w_s.at[0], w_r.at[0], along_x)
+        send(su, wsh.at[own_rows, SH : 2 * SH], w_s.at[1], w_r.at[1], along_y)
 
     accg[...] = jnp.zeros_like(accg)
     accu[...] = jnp.zeros_like(accu)
@@ -161,7 +165,6 @@
     drain(meta_all.at[pl.ds(0, LOC - 1)], mr)
     ids = jnp.concatenate([meta_all[b, 0:8, :] for b in range(LOC)], axis=1)
     gws = jnp.concatenate([meta_all[b, 8:16, :] for b in range(LOC)], axis=1)
-    ids_all[...] = ids
     expert = (lax.broadcasted_iota(jnp.int32, (GRP, COL), 0) * LOC + l).astype(F32)
     named = jnp.zeros((GRP, COL), F32)
     gate = jnp.zeros((GRP, COL), F32)
@@ -193,12 +196,18 @@
 
     def exchange(s):
         drain(xall.at[s, pl.ds(0, 4)], sib_r.at[s])
+        spot = s % RING
+        if not isinstance(s, int):
+
+            @pl.when(s >= RING)
+            def _():
+                drain(sbuf.at[spot, pl.ds(0, GRP - 1)], d_s.at[s - RING])
 
         def rows(i, carry):
             x = xall[s].reshape(COL, W)
             o = dot(onehot[pl.ds(pl.multiple_of(i * 4 * CAP, 4 * CAP), 4 * CAP), :], x)
             o = o.reshape(4, CAP, W)
-            sbuf[s, pl.ds(i * 4, 4)] = jnp.concatenate(
+            sbuf[spot, pl.ds(i * 4, 4)] = jnp.concatenate(
                 [o[:, :, :HALF], o[:, :, HALF:]], axis=1
             ).astype(BF16)
             return carry
@@ -206,22 +215,23 @@
         lax.fori_loop(0, GRP // 4, rows, 0)
         for step in ORDER:
             p = grp_partner(g, step)
-            send(sbuf.at[s, p], rbuf.at[s, g], d_s.at[s], d_r.at[s], (p, l))
-        pltpu.make_async_copy(sbuf.at[s, g], rbuf.at[s, g], d_l.at[s]).start()
+            send(sbuf.at[spot, p], rbuf.at[s, g], d_s.at[s], d_r.at[s], (p, l))
+        pltpu.make_async_copy(sbuf.at[spot, g], rbuf.at[s, g], d_l.at[s]).start()
 
     def cot_gather(s):
         cols = cot.at[:, pl.ds(pl.multiple_of(s * W, W), W)]
-        pltpu.make_async_copy(cols, cot_all.at[s, me], c_l.at[s]).start()
+        landing = cot_all.at[s, c, pl.ds(pl.multiple_of(z * T, T), T)]
+        pltpu.make_async_copy(cols, landing, c_l.at[s]).start()
         for dz in (1, 3, 2):
             send(
-                cols, cot_all.at[s, me], cg_s.at[s], cg_r.at[s],
+                cols, landing, cg_s.at[s], cg_r.at[s],
                 (g, loc_partner(z, c, dz, 0)[0]),
             )
 
     def cot_sibling(s):
-        drain(cot_all.at[s, pl.ds(0, 3)], cg_r.at[s])
-        drain(cot_all.at[s, 0], c_l.at[s])
-        mine = cot_all.at[s, pl.ds(c * 4, 4)]
+        drain(cot_all.at[s, 0, pl.ds(0, 3 * T)], cg_r.at[s])
+        drain(cot_all.at[s, 0, pl.ds(0, T)], c_l.at[s])
+        mine = cot_all.at[s, c]
         send(mine, mine, cs_s.at[s], cs_r.at[s], (g, sibling))
 
     def expert_in(s):
@@ -244,7 +254,21 @@
 
         lax.fori_loop(0, GRP // 4, rows, 0)
 
+    def pass_shards():
+        for copy in shard_copies:
+            copy.wait()
+        drain(wsh.at[pl.ds(0, 3 * SHARD), 0:SH], w_r.at[0])
+        drain(wsh.at[pl.ds(0, 3 * SHARD), SH : 2 * SH], w_r.at[1])
+        line = wsh.at[pl.ds(pl.multiple_of((g // 4) * 4 * SHARD, SHARD), 4 * SHARD), 0:SH]
+        for d in (1, 3, 2):
+            send(line, line, w_s.at[3], w_r.at[3], (grp_partner(g, (d, 0)), l))
+            for y in range(4):
+                first = pl.multiple_of((y * 4 + g % 4) * SHARD, SHARD)
+                piece = wsh.at[pl.ds(first, SHARD), SH : 2 * SH]
+                send(piece, piece, w_s.at[4], w_r.at[4], (grp_partner(g, (0, d)), l))
+
     to_sibling(0)
+    pass_shards()
     exchange(0)
     to_sibling(1)
 
@@ -268,14 +292,12 @@
 
     lax.fori_loop(0, NS - 1, step, 0)
     for st in ORDER:
-        send(sd, sd_all.at[own_rows], w_s.at[2], w_r.at[2], (grp_partner(g, st), l))
+        send(sd, sda.at[own_rows], w_s.at[2], w_r.at[2], (grp_partner(g, st), l))
     cot_gather(NS - 1)
     cot_sibling(NS - 2)
 
-    for copy in shard_copies:
-        copy.wait()
-    drain(wsh.at[pl.ds(0, D - SHARD), 0:SH], w_r.at[0])
-    drain(wsh.at[pl.ds(0, D - SHARD), SH : 2 * SH], w_r.at[1])
+    drain(wsh.at[pl.ds(0, 12 * SHARD), 0:SH], w_r.at[3])
+    drain(wsh.at[pl.ds(0, 12 * SHARD), SH : 2 * SH], w_r.at[4])
 
     def shared_in(s, carry):
         w = wsh[pl.ds(pl.multiple_of(s * W, W), W), :]
@@ -288,7 +310,49 @@
     shared_hidden[...] = (silu(sacc[:, 0:SH]) * sacc[:, SH : 2 * SH]).astype(BF16)
 
     cot_sibling(NS - 1)
+
+    for i in range(4):
+        slots4[i] = slot[4 * i : 4 * i + 4, :]
+    gacc[...] = jnp.zeros_like(gacc)
+    row80 = lax.broadcasted_iota(jnp.int32, (SUP, COL), 0).astype(F32)
+    for cw, shift in ((cwa, 0.0), (cwb, float(SUP - CAP))):
+        for e in range(GRP):
+            hit = (row80 - shift) == slots[e : e + 1, :]
+            onehot[pl.ds(SUP * e, SUP), :] = jnp.where(hit, gates[e : e + 1, :], 0.0).astype(BF16)
+        for j in range(GRP * SUP // T):
+            block = onehot[pl.ds(T * j, T), :].astype(F32)
+            cw[:, pl.ds(T * j, T)] = block.T.astype(BF16)
+
+    def back_weights(s):
+        cols = pl.ds(pl.multiple_of(s * W, W), W)
+        spot = (s + 1) % 2
+        return [
+            pltpu.make_async_copy(
+                wd.at[0, h * W : (h + 1) * W, cols],
+                wgb.at[spot, :, h * W : (h + 1) * W],
+                hbm.at[0, spot],
+            )
+            for h in range(2)
+        ]
+
+    def cotangents(s):
+        spot = (s + 1) % 2
+        return [
+            pltpu.make_async_copy(
+                cot_all.at[s, h], wub.at[spot, :, h * W : (h + 1) * W], hbm.at[1, spot]
+            )
+            for h in range(2)
+        ]
+
+    for copy in back_weights(0):
+        copy.start()
     expert_in(NS - 1)
+    for st in ORDER:
+        pl.semaphore_signal(
+            free, inc=1, device_id=(grp_partner(g, st), l), device_id_type=MESH
+        )
+    for copy in back_weights(1):
+        copy.start()
 
     def activate(i, carry):
         h = silu(accg[pl.ds(i * 2, 2)]) * accu[pl.ds(i * 2, 2)]
@@ -298,88 +362,61 @@
     lax.fori_loop(0, GRP // 2, activate, 0)
 
     drain(meta_all.at[pl.ds(0, LOC - 1)], ms)
-    drain(wsh.at[pl.ds(0, D - SHARD), 0:SH], w_s.at[0])
-    drain(wsh.at[pl.ds(0, D - SHARD), SH : 2 * SH], w_s.at[1])
-    drain(sd_all.at[pl.ds(0, D - SHARD)], w_s.at[2])
-    drain(sd_all.at[pl.ds(0, D - SHARD)], w_r.at[2])
-
-    def finish(s, carry):
+    drain(wsh.at[pl.ds(0, 3 * SHARD), 0:SH], w_s.at[0])
+    drain(wsh.at[pl.ds(0, 3 * SHARD), SH : 2 * SH], w_s.at[1])
+    drain(wsh.at[pl.ds(0, 12 * SHARD), 0:SH], w_s.at[3])
+    drain(wsh.at[pl.ds(0, 12 * SHARD), SH : 2 * SH], w_s.at[4])
+
+    def sent(s, carry):
         drain(xall.at[s, pl.ds(0, 3)], ag_s.at[s])
         drain(xall.at[s, pl.ds(0, 4)], sib_s.at[s])
-        drain(cot_all.at[s, pl.ds(0, 3)], cg_s.at[s])
-        drain(cot_all.at[s, pl.ds(0, 4)], cs_s.at[s])
-        drain(cot_all.at[s, pl.ds(0, 4)], cs_r.at[s])
-        drain(sbuf.at[s, pl.ds(0, GRP - 1)], d_s.at[s])
-        return carry
-
-    lax.fori_loop(0, NS, finish, 0)
-
-
-def return_kernel(
-    hidden, shared_hidden, slots, gates, ids_all, cot_all, sd_all, wd,
-    out, gg,
-    cwa, cwb, ohw, slots4, gacc, wdb, cotb, osend, orecv, psend, rrecv, sda, ggs, ggr,
-    o_s, o_r, o_l, p_s, p_r, w_l, g_s, g_r, hbm, cot_sem,
-):
-    g, l, z, c = place()
-    me = c * 4 + z
-    barrier = enter(g, l, z, c)
-
-    def weights(s, slot):
-        cols = pl.ds(pl.multiple_of(s * W, W), W)
-        return pltpu.make_async_copy(wd.at[0, :, cols], wdb.at[slot], hbm.at[slot])
-
-    def cotangents(s, slot):
-        return pltpu.make_async_copy(cot_all.at[s], cotb.at[slot], cot_sem.at[slot])
-
-    weights(0, 0).start()
-    weights(1, 1).start()
-    cotangents(0, 0).start()
-    shared_down = pltpu.make_async_copy(sd_all, sda, w_l)
-    shared_down.start()
+        drain(cot_all.at[s, 0, pl.ds(0, 3 * T)], cg_s.at[s])
+        drain(cot_all.at[s, 0], cs_s.at[s])
+        drain(cot_all.at[s, 0], cs_r.at[s])
+        return carry
+
+    lax.fori_loop(0, NS, sent, 0)
+    for s_last in range(NS - RING, NS):
+        drain(sbuf.at[s_last % RING, pl.ds(0, GRP - 1)], d_s.at[s_last])
+    for copy in cotangents(0):
+        copy.start()
 
     def expert_out(s):
-        slot_now = s % 2
-        weights(s, slot_now).wait()
+        spot, slot_now = s % RING, (s + 1) % 2
+        drain(wgb.at[slot_now], hbm.at[0, slot_now])
+        if not isinstance(s, int):
+
+            @pl.when(s >= RING)
+            def _():
+                drain(sbuf.at[spot, pl.ds(0, GRP - 1)], o_s.at[s - RING])
 
         def rows(i, carry):
-            h = hidden[pl.ds(pl.multiple_of(i * 4 * CAP, 4 * CAP), 4 * CAP), :]
-            o = dot(h, wdb[slot_now]).reshape(4, CAP, W)
-            osend[s, pl.ds(i * 4, 4)] = jnp.concatenate(
+            r = pl.ds(pl.multiple_of(i * 4 * CAP, 4 * CAP), 4 * CAP)
+            o = dot(hidden[r, 0:W], wgb[slot_now, :, 0:W])
+            o = o + dot(hidden[r, W : 2 * W], wgb[slot_now, :, W : 2 * W])
+            o = o.reshape(4, CAP, W)
+            sbuf[spot, pl.ds(i * 4, 4)] = jnp.concatenate(
                 [o[:, :, :HALF], o[:, :, HALF:]], axis=1
             ).astype(BF16)
             return carry
 
         lax.fori_loop(0, GRP // 4, rows, 0)
-        for step in ORDER:
-            p = grp_partner(g, step)
-            send(osend.at[s, p], orecv.at[s, g], o_s.at[s], o_r.at[s], (p, l))
-        pltpu.make_async_copy(osend.at[s, g], orecv.at[s, g], o_l.at[s]).start()
-
-    pl.semaphore_wait(barrier, len(ORDER) + len(LOC_STEPS))
+        if isinstance(s, int) and s == 0:
+            pl.semaphore_wait(free, len(ORDER))
+        for st in ORDER:
+            p = grp_partner(g, st)
+            send(sbuf.at[spot, p], rbuf.at[s, g], o_s.at[s], o_r.at[s], (p, l))
+        pltpu.make_async_copy(sbuf.at[spot, g], rbuf.at[s, g], o_l.at[s]).start()
+
     expert_out(0)
-
-    slot = slots[...]
-    gate = gates[...]
-    for i in range(4):
-        slots4[i] = slot[4 * i : 4 * i + 4, :]
-    gacc[...] = jnp.zeros_like(gacc)
-    row = lax.broadcasted_iota(jnp.int32, (SUP, COL), 0).astype(F32)
-    for cw, shift in ((cwa, 0.0), (cwb, float(SUP - CAP))):
-        for e in range(GRP):
-            hit = (row - shift) == slot[e : e + 1, :]
-            ohw[pl.ds(SUP * e, SUP), :] = jnp.where(hit, gate[e : e + 1, :], 0.0).astype(BF16)
-        for j in range(GRP * SUP // T):
-            block = ohw[pl.ds(T * j, T), :].astype(F32)
-            cw[:, pl.ds(T * j, T)] = block.T.astype(BF16)
-
     expert_out(1)
-    shared_down.wait()
+    drain(sda.at[pl.ds(0, D - SHARD)], w_r.at[2])
+    drain(sda.at[pl.ds(0, D - SHARD)], w_s.at[2])
 
     def combine(s):
-        slot_now = s % 2
-        drain(orecv.at[s, pl.ds(0, GRP - 1)], o_r.at[s])
-        drain(orecv.at[s, 0], o_l.at[s])
+        slot_now = (s + 1) % 2
+        drain(rbuf.at[s, pl.ds(0, GRP - 1)], o_r.at[s])
+        drain(rbuf.at[s, 0], o_l.at[s])
         for half in range(2):
             first = 0 if half == 0 else PACK - SUP
             cw = cwa if half == 0 else cwb
@@ -387,33 +424,33 @@
             cols = slice(half * HALF, (half + 1) * HALF)
 
             def tokens(i, carry):
-                y = orecv[s, :, first : first + SUP, :].reshape(GRP * SUP, HALF)
+                y = rbuf[s, :, first : first + SUP, :].reshape(GRP * SUP, HALF)
                 rows = pl.ds(pl.multiple_of(i * 256, 256), 256)
                 part = dot(cw[rows, :], y) + dot_nt(shared_hidden[rows, :], sda[rows_sd, :])
-                psend[s, pl.ds(i * 2, 2), :, cols] = part.reshape(2, T, HALF).astype(BF16)
+                xall[s, pl.ds(i * 2, 2), :, cols] = part.reshape(2, T, HALF).astype(BF16)
                 return carry
 
             lax.fori_loop(0, COL // 256, tokens, 0)
             for dz, dc in LOC_STEPS:
                 pl_, blk = loc_partner(z, c, dz, dc)
                 send(
-                    psend.at[s, blk, :, cols], rrecv.at[s, me, :, cols], p_s.at[s], p_r.at[s],
+                    xall.at[s, blk, :, cols], rrecv.at[s, me, :, cols], p_s.at[s], p_r.at[s],
                     (g, pl_),
                 )
-        rrecv[s, me] = psend[s, me]
-
-        cotangents(s, slot_now).wait()
+        rrecv[s, me] = xall[s, me]
+
+        drain(wub.at[slot_now], hbm.at[1, slot_now])
         for half in range(2):
             first = 0 if half == 0 else PACK - SUP
             shift = 0.0 if half == 0 else float(SUP - CAP)
             cols = slice(half * HALF, (half + 1) * HALF)
 
             def products(i, carry):
-                y = orecv[s, pl.ds(i * 4, 4), first : first + SUP, :].reshape(4 * SUP, HALF)
+                y = rbuf[s, pl.ds(i * 4, 4), first : first + SUP, :].reshape(4 * SUP, HALF)
                 pos = lax.broadcasted_iota(jnp.int32, (SUP, COL // 2), 0).astype(F32) - shift
                 for h in range(2):
                     tok = slice(h * COL // 2, (h + 1) * COL // 2)
-                    ct = cotb[slot_now, pl.ds(h * 4, 4), :, cols].reshape(COL // 2, HALF)
+                    ct = wub[slot_now, :, h * W + half * HALF : h * W + (half + 1) * HALF]
                     prod = dot_nt(y, ct).reshape(4, SUP, COL // 2)
                     sl = slots4[i, :, tok]
                     sums = [
@@ -434,14 +471,16 @@
             acc = acc + rrecv[s, b].astype(F32)
         out[:, pl.ds(pl.multiple_of(s * W, W), W)] = acc.astype(BF16)
 
-    def step(s, carry):
+    def back_step(s, carry):
         @pl.when(s + 1 < NS)
         def _():
-            cotangents(s + 1, (s + 1) % 2).start()
+            for copy in cotangents(s + 1):
+                copy.start()
 
         @pl.when(s + 2 < NS)
         def _():
-            weights(s + 2, s % 2).start()
+            for copy in back_weights(s + 2):
+                copy.start()
 
         combine(s)
 
@@ -455,9 +494,8 @@
 
         return carry
 
-    lax.fori_loop(0, NS, step, 0)
-
-    ids = ids_all[...]
+    lax.fori_loop(0, NS, back_step, 0)
+
     grads = jnp.zeros((8, COL), F32)
     for i in range(4):
         block = gacc[i]
@@ -480,11 +518,12 @@
     drain(ggs.at[pl.ds(0, LOC - 1)], g_s)
 
     def finish(s, carry):
-        drain(osend.at[s, pl.ds(0, GRP - 1)], o_s.at[s])
-        drain(psend.at[s, pl.ds(0, LOC - 1)], p_s.at[s])
+        drain(xall.at[s, pl.ds(0, LOC - 1)], p_s.at[s])
         return carry
 
     lax.fori_loop(0, NS, finish, 0)
+    for s_last in range(NS - RING, NS):
+        drain(sbuf.at[s_last % RING, pl.ds(0, GRP - 1)], o_s.at[s_last])
 
 
 def body(
@@ -494,23 +533,19 @@
     vm = pl.BlockSpec(memory_space=pltpu.VMEM)
     hb = pl.BlockSpec(memory_space=pl.ANY)
     dma = pltpu.SemaphoreType.DMA
-    hidden, shared_hidden, slots, gates, ids_all, cot_all, sd_all = pl.pallas_call(
-        dispatch_kernel,
+    out, grads, _ = pl.pallas_call(
+        layer_kernel,
         out_shape=(
-            jax.ShapeDtypeStruct((GRP * CAP, FF), BF16),
-            jax.ShapeDtypeStruct((COL, SH), BF16),
-            jax.ShapeDtypeStruct((GRP, COL), F32),
-            jax.ShapeDtypeStruct((GRP, COL), F32),
-            jax.ShapeDtypeStruct((8, COL), F32),
-            jax.ShapeDtypeStruct((NS, LOC, T, W), BF16),
-            jax.ShapeDtypeStruct((D, SH), BF16),
+            jax.ShapeDtypeStruct((T, D), BF16),
+            jax.ShapeDtypeStruct((8, T), F32),
+            jax.ShapeDtypeStruct((NS, 2, COL // 2, W), BF16),
         ),
-        in_specs=[vm] * 8 + [hb] * 2,
-        out_specs=(vm,) * 5 + (hb,) * 2,
+        in_specs=[vm] * 8 + [hb] * 3,
+        out_specs=(vm, vm, hb),
         scratch_shapes=[
             pltpu.VMEM((NS, LOC, T, W), BF16),
-            pltpu.VMEM((GRP * CAP, COL), BF16),
-            pltpu.VMEM((NS, GRP, PACK, HALF), BF16),
+            pltpu.VMEM((GRP * SUP, COL), BF16),
+            pltpu.VMEM((RING, GRP, PACK, HALF), BF16),
             pltpu.VMEM((NS, GRP, PACK, HALF), BF16),
             pltpu.VMEM((GRP, CAP, FF), F32),
             pltpu.VMEM((GRP, CAP, FF), F32),
@@ -519,51 +554,33 @@
             pltpu.VMEM((D, 2 * SH), BF16),
             pltpu.VMEM((COL, 2 * SH), F32),
             pltpu.VMEM((LOC, 16, T), F32),
+            pltpu.VMEM((GRP * CAP, FF), BF16),
+            pltpu.VMEM((COL, SH), BF16),
+            pltpu.VMEM((GRP, COL), F32),
+            pltpu.VMEM((GRP, COL), F32),
+            pltpu.VMEM((D, SH), BF16),
+            pltpu.VMEM((COL, GRP * SUP), BF16),
+            pltpu.VMEM((COL, GRP * SUP), BF16),
+            pltpu.VMEM((4, 4, COL), F32),
+            pltpu.VMEM((4, 4, COL), F32),
+            pltpu.VMEM((NS, LOC, T, W), BF16),
+            pltpu.VMEM((LOC, 8, T), F32),
+            pltpu.VMEM((LOC, 8, T), F32),
         ]
-        + [dma(()), dma(())]
-        + [dma((NS,))] * 12
-        + [dma((3,))] * 3
+        + [dma(())] * 4
+        + [pltpu.SemaphoreType.REGULAR]
+        + [dma((NS,))] * 17
+        + [dma((5,))] * 2
+        + [dma((3,))]
         + [dma((2, 2))],
         compiler_params=pltpu.CompilerParams(
             collective_id=0, has_side_effects=True, vmem_limit_bytes=VMEM_LIMIT
         ),
-        name="dispatch",
+        name="layer",
     )(
         stream_in, norm_gain, expert_ids.T, gate_weights.T, shared_gate, shared_up, shared_down.T,
-        cotangent, expert_gate, expert_up,
+        cotangent, expert_gate, expert_up, expert_down,
     )
-    out, grads = pl.pallas_call(
-        return_kernel,
-        out_shape=(
-            jax.ShapeDtypeStruct((T, D), BF16),
-            jax.ShapeDtypeStruct((8, T), F32),
-        ),
-        in_specs=[vm] * 5 + [hb] * 3,
-        out_specs=(vm, vm),
-        scratch_shapes=[
-            pltpu.VMEM((COL, GRP * SUP), BF16),
-            pltpu.VMEM((COL, GRP * SUP), BF16),
-            pltpu.VMEM((GRP * SUP, COL), BF16),
-            pltpu.VMEM((4, 4, COL), F32),
-            pltpu.VMEM((4, 4, COL), F32),
-            pltpu.VMEM((2, FF, W), BF16),
-            pltpu.VMEM((2, LOC, T, W), BF16),
-            pltpu.VMEM((NS, GRP, PACK, HALF), BF16),
-            pltpu.VMEM((NS, GRP, PACK, HALF), BF16),
-            pltpu.VMEM((NS, LOC, T, W), BF16),
-            pltpu.VMEM((NS, LOC, T, W), BF16),
-            pltpu.VMEM((D, SH), BF16),
-            pltpu.VMEM((LOC, 8, T), F32),
-            pltpu.VMEM((LOC, 8, T), F32),
-        ]
-        + [dma((NS,))] * 5
-        + [dma(())] * 3
-        + [dma((2,))] * 2,
-        compiler_params=pltpu.CompilerParams(
-            collective_id=1, has_side_effects=True, vmem_limit_bytes=VMEM_LIMIT
-        ),
-        name="give_back",
-    )(hidden, shared_hidden, slots, gates, ids_all, cot_all, sd_all, expert_down)
     return out, grads.T
 
 

time: 262 us -> 248 us (0.947); the launches traced: 257 us -> 248 us
  Pallas kernels: 253 us -> 244 us
    pallas_call x2 -> x1, Pallas kernels: 253 us -> 244 us  [body(): pl.pallas_call(layer_kernel, out_shape=(jax.ShapeDtypeStruct((T, D), BF16...]
where the time goes in v3:
time: 248 us
  Pallas kernels  244 us (98%)
  local copies, waits for them, and re-layouts  3.43 us (1%)
    pallas_call x1, Pallas kernels, body(): pl.pallas_call(layer_kernel, out_shape=(jax.ShapeDtypeStruct((T, D), BF16...  244 us

profile of v3, /device:TPU:1, one launch (start us, length us, event | category | flops | bytes accessed | tf_op | source)
XLA Modules:
  0.0 247.8 jit_solution(7337071548978626073)
XLA Ops:
  0.6 243.7 %layer.1 = (bf16[128,3584]{1,0:T(8,128)(2,1)}, f32[8,128]{1,0:T(8,128)}, bf16[7,2,512,512]{3,2,1,0:T(8,128)(2,1)}) custom-call(bf16[128,3584]{1,0:T(8,128)(2,1)} %stream.1, f32[3584]{0:T(1024)} %gain.1, s32[8,128]{1,0:T(8,128)} %bitcast.6, bf16[8,128]{1,0:T(8,128)(2,1)} %bitcast.7, bf16[224,128]{1,0:T(8,128)(2,1)} %sg.1, bf16[224,128]{1,0:T(8,128)(2,1)} %su.1, ...), custom_call_target="tpu_custom_call" | custom-call | tf_op jit(solution)/shard_map/layer/pallas_call | solution.py:536
  244.4 2.2 copy.15
  246.5 1.3 copy.16

commit v4 on v3

--- a/solution.py
+++ b/solution.py
@@ -524,6 +524,11 @@
     lax.fori_loop(0, NS, finish, 0)
     for s_last in range(NS - RING, NS):
         drain(sbuf.at[s_last % RING, pl.ds(0, GRP - 1)], o_s.at[s_last])
+
+
+def results(out, grads, out_copy, grads_copy):
+    out_copy[...] = out[...]
+    grads_copy[...] = grads[...]
 
 
 def body(
@@ -581,6 +586,13 @@
         stream_in, norm_gain, expert_ids.T, gate_weights.T, shared_gate, shared_up, shared_down.T,
         cotangent, expert_gate, expert_up, expert_down,
     )
+    out, grads = pl.pallas_call(
+        results,
+        out_shape=(jax.ShapeDtypeStruct((T, D), BF16), jax.ShapeDtypeStruct((8, T), F32)),
+        in_specs=[vm, vm],
+        out_specs=(vm, vm),
+        name="results",
+    )(out, grads)
     return out, grads.T
 
 

time: 248 us -> 247 us (level)
  local copies, waits for them, and re-layouts: 3.43 us -> 0 us
    unnamed x2 -> x0, local copies, waits for them, and re-layouts: 3.43 us -> none
where the time goes in v4:
time: 247 us
  Pallas kernels  246 us (100%)
    pallas_call x1, Pallas kernels, body(): pl.pallas_call(layer_kernel, out_shape=(jax.ShapeDtypeStruct((T, D), BF16...  244 us

profile of v4, /device:TPU:1, one launch (start us, length us, event | category | flops | bytes accessed | tf_op | source)
XLA Modules:
  0.0 246.5 jit_solution(15888866238578500049)
XLA Ops:
  0.6 243.7 %layer.1 = (bf16[128,3584]{1,0:T(8,128)(2,1)}, f32[8,128]{1,0:T(8,128)}, bf16[7,2,512,512]{3,2,1,0:T(8,128)(2,1)}) custom-call(bf16[128,3584]{1,0:T(8,128)(2,1)} %stream.1, f32[3584]{0:T(1024)} %gain.1, s32[8,128]{1,0:T(8,128)} %bitcast.5, bf16[8,128]{1,0:T(8,128)(2,1)} %bitcast.6, bf16[224,128]{1,0:T(8,128)(2,1)} %sg.1, bf16[224,128]{1,0:T(8,128)(2,1)} %su.1, ...), custom_call_target="tpu_custom_call" | custom-call | tf_op jit(solution)/shard_map/layer/pallas_call | solution.py:541
  244.4 2.2 results.1
